TPU v7x, 32 devices: a whole 2x2x4 slice. The times are simulated.
32 devices in a mesh: row: 8 (over y, x, core), col: 4 (over z).
Axes of the slice: x: 2, y: 2, z: 4, core: 2. Of those that a mesh axis runs over, the one named last changes fastest.
Arguments:
- matrix: float32 [8192, 2048], P('row', 'col'), may hold values from -100 to 100, as said below
Outputs:
- updated: float32 [8192, 2048], P('row', 'col')
- top: float32 [128, 2048], P(None, 'col')
Inputs may be any that keep to these rules, and one draw needn't show every extreme that they name: The first 128 columns of matrix have full column rank.
All inputs are finite; a program needn't handle non-finite values.
Results may differ from a plain program's by a relative error of at most 0.0006.
Values sent between devices are 32-bit elements; how exact they have to be, the bound alone decides.
A program may use at most 64 MiB of HBM per device.

v0:
```python
import functools
import math

import jax
import jax.numpy as jnp
from jax import lax
from jax.experimental import pallas as pl
from jax.experimental.pallas import tpu as pltpu
from jax.sharding import PartitionSpec as P

B = 128
S = 8
CHUNKS = 8
HI = lax.Precision.HIGHEST


def mm(left, right, dims):
    return lax.dot_general(
        left, right, (dims, ((), ())), precision=HI, preferred_element_type=jnp.float32
    )


def factor_steps(w_ref, low, high, state=None, after_step=None):
    lane = lax.broadcasted_iota(jnp.int32, (S, B), 1)
    sub = lax.broadcasted_iota(jnp.int32, (S, B), 0)
    wide = lax.broadcasted_iota(jnp.int32, (B - 2 * S, B), 1)

    def step(k, state):
        rows, mult, last = state
        d = {}
        for j in range(S):
            column = jnp.broadcast_to(rows[:, j : j + 1], (S, B))
            for i in range(j, S):
                d[i, j] = jnp.broadcast_to(column[i : i + 1], (S, B))
        rest = w_ref[S : B - S] - mm(mult, last, ((0,), (0,)))[2 * S :]
        rest = pltpu.roll(jnp.where(wide < S, 0.0, rest), B - S, 1)
        w_ref[: B - 2 * S] = rest
        w_ref[B - 2 * S : B - S] = pltpu.roll(jnp.where(lane < S, 0.0, last), B - S, 1)
        rows = jnp.where(lane < S, jnp.where(lane == sub, 1.0, 0.0), rows)
        p = [jnp.broadcast_to(rows[j : j + 1], (S, B)) for j in range(S)]
        t = None
        for j in range(S):
            inv = lax.rsqrt(d[j, j])
            l = {i: d[i, j] * inv for i in range(j + 1, S)}
            for i in range(j + 1, S):
                for m in range(j + 1, i + 1):
                    d[i, m] = d[i, m] - l[i] * l[m]
            tj = p[j] * inv
            for i in range(j + 1, S):
                p[i] = p[i] - l[i] * tj
            t = tj if t is None else jnp.where(sub == j, tj, t)
        mult = jnp.where((lane >= S) & (lane < B - S * k), t, 0.0)
        last = pltpu.roll(t, B - S, 1)
        after = rest[:S]
        for i in range(S):
            column = jnp.broadcast_to(mult[:, S + i : S + i + 1], (S, B))
            drop = jnp.sum(column * last, axis=0, keepdims=True)
            after = jnp.where(sub == i, after - drop, after)
        if after_step is not None:
            after_step(k)
        return after, mult, last

    if low == 0:
        state = (w_ref[:S], jnp.zeros((S, B), jnp.float32), w_ref[B - S :])
    state = lax.fori_loop(low, high, step, state)
    if high == B // S:
        w_ref[B - S :] = state[2]
    return state


class Sum:
    def __init__(self, size, me, src, box, full, sems):
        self.size, self.me, self.src, self.box, self.full = size, me, src, box, full
        self.sems = sems
        self.slab = max(8, B // size)
        self.owners = B // self.slab

    def rows(self, owner):
        return pl.ds(pl.multiple_of(owner * self.slab, self.slab), self.slab)

    def own(self, device, what):
        if self.owners == self.size:
            what()
        else:
            pl.when(device < self.owners)(what)

    def scatter_copy(self, i):
        peer = self.me ^ i
        return pltpu.make_async_remote_copy(
            src_ref=self.src.at[self.rows(peer)],
            dst_ref=self.box.at[i],
            send_sem=self.sems.at[0, i],
            recv_sem=self.sems.at[1, i],
            device_id={"row": peer},
            device_id_type=pl.DeviceIdType.MESH,
        )

    def scatter_from(self, i):
        return pltpu.make_async_remote_copy(
            src_ref=self.box.at[i],
            dst_ref=self.box.at[i],
            send_sem=self.sems.at[0, i],
            recv_sem=self.sems.at[1, i],
            device_id={"row": self.me ^ i},
            device_id_type=pl.DeviceIdType.MESH,
        )

    def gather_copy(self, i, owner):
        return pltpu.make_async_remote_copy(
            src_ref=self.full.at[self.rows(owner)],
            dst_ref=self.full.at[self.rows(owner)],
            send_sem=self.sems.at[2, i],
            recv_sem=self.sems.at[3, i],
            device_id={"row": self.me ^ i},
            device_id_type=pl.DeviceIdType.MESH,
        )

    def start(self):
        for i in range(1, self.size):
            self.own(self.me ^ i, lambda: self.scatter_copy(i).start())

    def middle(self):
        for i in range(1, self.size):
            self.own(self.me ^ i, lambda: self.scatter_copy(i).wait_send())

        def add():
            total = self.src[self.rows(self.me)]
            for i in range(1, self.size):
                self.scatter_from(i).wait_recv()
                total = total + self.box[i]
            self.full[self.rows(self.me)] = total
            self.box[0] = total

        self.own(self.me, add)

    def spread(self):
        def send():
            for i in range(1, self.size):
                self.gather_copy(i, self.me).start()

        self.own(self.me, send)

    def end(self):
        for i in range(1, self.size):
            self.own(self.me ^ i, lambda: self.gather_copy(i, self.me ^ i).wait_recv())

    def drain(self):
        def sent():
            for i in range(1, self.size):
                self.gather_copy(i, self.me).wait_send()

        self.own(self.me, sent)


def kernel(
    nrow, ncol, m_hbm, q_v, g2_v, p_v,
    m_v, a_v, s1_v, s2_v, sp_v, g1_v, box1, box2, boxp,
    in_sems, chain_sems, g_sems, sems1, sems2, semsp,
):
    me = lax.axis_index("row")
    z = lax.axis_index("col")
    height = m_v.shape[0]
    part = height // CHUNKS
    load_m = pltpu.make_async_copy(m_hbm, m_v, in_sems.at[0])
    load_a = pltpu.make_async_copy(m_hbm.at[:, pl.ds(0, B)], a_v, in_sems.at[1])

    barrier = pltpu.get_barrier_semaphore()
    for i in range(1, nrow):
        pl.semaphore_signal(
            barrier, inc=1, device_id={"row": me ^ i}, device_id_type=pl.DeviceIdType.MESH
        )
    for i in range(1, ncol):
        pl.semaphore_signal(
            barrier, inc=1, device_id={"col": z ^ i}, device_id_type=pl.DeviceIdType.MESH
        )

    pl.when(z == 0)(load_a.start)
    load_m.start()
    pl.semaphore_wait(barrier, nrow + ncol - 2)

    def chain(c):
        block = a_v.at[pl.ds(pl.multiple_of(c * part, part), part)]
        return pltpu.make_async_remote_copy(
            src_ref=block,
            dst_ref=block,
            send_sem=chain_sems.at[0, c],
            recv_sem=chain_sems.at[1, c],
            device_id={"col": lax.rem(z + 1, ncol)},
            device_id_type=pl.DeviceIdType.MESH,
        )

    passes_on = (z > 0) & (z < ncol - 1)

    def forward(c):
        chain(c).wait_recv()
        chain(c).start()

    first = Sum(nrow, me, s1_v, box1, g1_v, sems1)
    second = Sum(nrow, me, s2_v, box2, g2_v, sems2)
    coeffs = Sum(nrow, me, sp_v, boxp, p_v, semsp)

    def hand(which, total, i):
        return pltpu.make_async_remote_copy(
            src_ref=total.box.at[0],
            dst_ref=total.full.at[total.rows(me)],
            send_sem=g_sems.at[2 * which, i],
            recv_sem=g_sems.at[2 * which + 1, 0],
            device_id={"col": i},
            device_id_type=pl.DeviceIdType.MESH,
        )

    def give(which, total):
        def send():
            for i in range(1, ncol):
                hand(which, total, i).start()

        first.own(me, send)

    @pl.when(z == 0)
    def _():
        load_a.wait()
        for c in range(3):
            chain(c).start()
        s1_v[...] = mm(a_v[...], a_v[...], ((0,), (0,)))
        first.start()
        first.middle()
        give(0, first)
        first.spread()
        for c in range(3, CHUNKS):
            chain(c).start()

    @pl.when(passes_on)
    def _():
        for c in range(4):
            forward(c)

    @pl.when(z > 0)
    def _():
        first.own(me, lambda: hand(0, first, 0).wait_recv())
        first.spread()

    first.end()
    first.drain()

    def pass_on(k):
        @pl.when(passes_on & (k % 3 == 1) & (k < 12))
        def _():
            forward(4 + k // 3)

    factor_steps(g1_v, 0, B // S, None, pass_on)

    big = 2 * part

    @pl.when(z == 0)
    def _():
        for c in range(CHUNKS // 2):
            rows = pl.ds(c * big, big)
            q_v[rows] = mm(a_v[rows], g1_v[...], ((1,), (1,)))
        q = q_v[...]
        s2_v[...] = mm(q, q, ((0,), (0,)))
        second.start()
        load_m.wait()
        sp_v[...] = mm(q_v[...], m_v[...], ((0,), (0,)))
        second.middle()
        give(1, second)
        second.spread()
        coeffs.start()

    @pl.when(z > 0)
    def _():
        load_m.wait()
        for c in range(CHUNKS // 2):
            if c == CHUNKS // 2 - 1:
                second.own(me, lambda: hand(1, second, 0).wait_recv())
                second.spread()

            @pl.when(z == ncol - 1)
            def _():
                chain(2 * c).wait_recv()
                chain(2 * c + 1).wait_recv()

            rows = pl.ds(c * big, big)
            q = mm(a_v[rows], g1_v[...], ((1,), (1,)))
            q_v[rows] = q
            term = mm(q, m_v[rows], ((0,), (0,)))
            if c == 0:
                sp_v[...] = term
            else:
                sp_v[...] += term
        coeffs.start()

    second.end()
    second.drain()
    state = factor_steps(g2_v, 0, B // S // 2)
    coeffs.middle()
    coeffs.spread()
    factor_steps(g2_v, B // S // 2, B // S, state)
    coeffs.end()
    coeffs.drain()

    @pl.when(z == 0)
    def _():
        def given():
            for i in range(1, ncol):
                hand(0, first, i).wait_send()
                hand(1, second, i).wait_send()

        first.own(me, given)

    @pl.when(z < ncol - 1)
    def _():
        for c in range(CHUNKS):
            chain(c).wait_send()


def halves(x):
    high = x.astype(jnp.bfloat16)
    return high, (x - high.astype(jnp.float32)).astype(jnp.bfloat16)


def project_kernel(rows, m_ref, q_ref, g2_ref, p_ref, out_hbm, top_ref, out_v, back_v, sems):
    height, width = m_ref.shape
    part = height // 4
    scale = math.sqrt(rows)
    on_panel = lax.axis_index("col") == 0
    g2 = g2_ref[...]
    c = mm(g2, p_ref[...], ((1,), (0,)))
    top_ref[...] = c / scale
    back = mm(g2, c, ((0,), (0,)))
    leading = jnp.where(on_panel, -scale * g2.T, back[:, :B])
    high, low = halves(jnp.concatenate([leading, back[:, B:]], 1))
    back_v[:B] = high
    back_v[B : 2 * B] = high
    back_v[2 * B :] = low

    def store(i):
        block = pl.ds(i * part, part)
        return pltpu.make_async_copy(out_v.at[block], out_hbm.at[block], sems.at[i])

    for i in range(4):
        block = pl.ds(i * part, part)
        high, low = halves(q_ref[block])
        change = jnp.dot(
            jnp.concatenate([high, low, high], 1), back_v[...], preferred_element_type=jnp.float32
        )
        base = m_ref[block]
        out_v[block, :B] = jnp.where(on_panel, 0.0, base[:, :B]) - change[:, :B]
        out_v[block, B:] = base[:, B:] - change[:, B:]
        store(i).start()
    for i in range(4):
        store(i).wait()


def on_device(nrow, ncol, matrix):
    height, width = matrix.shape
    slab = max(8, B // nrow)
    f32 = jnp.float32
    dma = pltpu.SemaphoreType.DMA
    shape = jax.ShapeDtypeStruct
    basis, inverse, coeffs = pl.pallas_call(
        functools.partial(kernel, nrow, ncol),
        out_shape=(shape((height, B), f32), shape((B, B), f32), shape((B, width), f32)),
        in_specs=[pl.BlockSpec(memory_space=pl.ANY)],
        out_specs=(pl.BlockSpec(memory_space=pltpu.VMEM),) * 3,
        scratch_shapes=[
            pltpu.VMEM((height, width), f32),
            pltpu.VMEM((height, B), f32),
            pltpu.VMEM((B, B), f32),
            pltpu.VMEM((B, B), f32),
            pltpu.VMEM((B, width), f32),
            pltpu.VMEM((B, B), f32),
            pltpu.VMEM((nrow, slab, B), f32),
            pltpu.VMEM((nrow, slab, B), f32),
            pltpu.VMEM((nrow, slab, width), f32),
            dma((2,)),
            dma((2, CHUNKS)),
            dma((4, ncol)),
            dma((4, nrow)),
            dma((4, nrow)),
            dma((4, nrow)),
        ],
        compiler_params=pltpu.CompilerParams(
            collective_id=0, has_side_effects=True, vmem_limit_bytes=60 * 2**20
        ),
    )(matrix)
    whole = pl.BlockSpec(memory_space=pltpu.VMEM)
    return pl.pallas_call(
        functools.partial(project_kernel, height * nrow),
        out_shape=(shape((height, width), f32), shape((B, width), f32)),
        in_specs=[whole] * 4,
        out_specs=(pl.BlockSpec(memory_space=pl.ANY), whole),
        scratch_shapes=[
            pltpu.VMEM((height, width), f32),
            pltpu.VMEM((3 * B, width), jnp.bfloat16),
            dma((4,)),
        ],
        compiler_params=pltpu.CompilerParams(vmem_limit_bytes=32 * 2**20),
    )(matrix, basis, inverse, coeffs)


def solution(mesh):
    nrow, ncol = mesh.shape["row"], mesh.shape["col"]
    return jax.shard_map(
        functools.partial(on_device, nrow, ncol),
        mesh=mesh,
        in_specs=(P("row", "col"),),
        out_specs=(P("row", "col"), P(None, "col")),
        check_vma=False,
    )
```

profile of v0, /device:TPU:17, one launch (start us, length us, event | category | flops | bytes accessed | tf_op | source)
XLA Modules:
  0.0 47.4 jit_solution(16198427379879092280)
XLA Ops:
  0.6 0.0 copy-start
  0.6 40.8 %shard_map.30 = (f32[1024,128]{1,0:T(8,128)}, f32[128,128]{1,0:T(8,128)}, f32[128,512]{1,0:T(8,128)}) custom-call(f32[1024,512]{1,0:T(8,128)} %m_ref.1), custom_call_target="tpu_custom_call" | custom-call | tf_op jit(solution)/shard_map/pallas_call | solution.py:360
  41.4 0.0 copy-done
  41.4 0.0 copy-start.1
  41.5 1.0 %copy-done.1 = f32[1024,128]{1,0:T(8,128)S(1)} copy-done((f32[1024,128]{1,0:T(8,128)S(1)}, f32[1024,128]{1,0:T(8,128)}, u32[]{:S(2)}) %copy-start.1) | copy-done | bytes 524312
  42.5 0.0 copy-start.2
  42.5 0.9 %copy-done.2 = f32[128,512]{1,0:T(8,128)S(1)} copy-done((f32[128,512]{1,0:T(8,128)S(1)}, f32[128,512]{1,0:T(8,128)}, u32[]{:S(2)}) %copy-start.2) | copy-done | bytes 262168
  43.4 0.0 copy-start.3
  43.4 0.8 %copy-done.3 = f32[128,128]{1,0:T(8,128)S(1)} copy-done((f32[128,128]{1,0:T(8,128)S(1)}, f32[128,128]{1,0:T(8,128)}, u32[]{:S(2)}) %copy-start.3) | copy-done | bytes 65560
  44.3 3.1 %shard_map.31 = (f32[1024,512]{1,0:T(8,128)}, f32[128,512]{1,0:T(8,128)}) custom-call(f32[1024,512]{1,0:T(8,128)S(1)} %copy-done, f32[1024,128]{1,0:T(8,128)S(1)} %copy-done.1, f32[128,128]{1,0:T(8,128)S(1)} %copy-done.3, f32[128,512]{1,0:T(8,128)S(1)} %copy-done.2), custom_call_target="tpu_custom_call" | custom-call | tf_op jit(solution)/shard_map/pallas_call | solution.py:387
Async XLA Ops:
  0.6 40.8 %copy-start = (f32[1024,512]{1,0:T(8,128)S(1)}, f32[1024,512]{1,0:T(8,128)}, u32[]{:S(2)}) copy-start(f32[1024,512]{1,0:T(8,128)} %m_ref.1) | copy-start | bytes 6291460
  41.4 1.0 %copy-start.1 = (f32[1024,128]{1,0:T(8,128)S(1)}, f32[1024,128]{1,0:T(8,128)}, u32[]{:S(2)}) copy-start(f32[1024,128]{1,0:T(8,128)} %get-tuple-element.5.q_ref) | copy-start | bytes 1572868
  42.5 0.9 %copy-start.2 = (f32[128,512]{1,0:T(8,128)S(1)}, f32[128,512]{1,0:T(8,128)}, u32[]{:S(2)}) copy-start(f32[128,512]{1,0:T(8,128)} %get-tuple-element.7.p_ref) | copy-start | bytes 786436
  43.4 0.8 %copy-start.3 = (f32[128,128]{1,0:T(8,128)S(1)}, f32[128,128]{1,0:T(8,128)}, u32[]{:S(2)}) copy-start(f32[128,128]{1,0:T(8,128)} %get-tuple-element.6.g2_ref) | copy-start | bytes 196612
where the time goes:
time: 47.6 us; the launch traced here: 47.4 us
  Pallas kernels  43.9 us (92%)
  local copies, waits for them, and re-layouts  2.83 us (6%)
  between operations  0.66 us (1%)
    pallas_call x1, Pallas kernels, on_device(): pl.pallas_call(functools.partial(kernel, nrow, ncol), out_shape=(shape((h...  40.8 us
    pallas_call x1, Pallas kernels, on_device(): pl.pallas_call(functools.partial(project_kernel, height * nrow), out_shap...  3.07 us
    unnamed x8, local copies, waits for them, and re-layouts  2.83 us

commit v1 on v0

--- a/solution.py
+++ b/solution.py
@@ -153,8 +153,8 @@
 
 
 def kernel(
-    nrow, ncol, m_hbm, q_v, g2_v, p_v,
-    m_v, a_v, s1_v, s2_v, sp_v, g1_v, box1, box2, boxp,
+    nrow, ncol, m_hbm, m_v, q_v, g2_v, p_v,
+    a_v, s1_v, s2_v, sp_v, g1_v, box1, box2, boxp,
     in_sems, chain_sems, g_sems, sems1, sems2, semsp,
 ):
     me = lax.axis_index("row")
@@ -357,13 +357,14 @@
     f32 = jnp.float32
     dma = pltpu.SemaphoreType.DMA
     shape = jax.ShapeDtypeStruct
-    basis, inverse, coeffs = pl.pallas_call(
+    held, basis, inverse, coeffs = pl.pallas_call(
         functools.partial(kernel, nrow, ncol),
-        out_shape=(shape((height, B), f32), shape((B, B), f32), shape((B, width), f32)),
-        in_specs=[pl.BlockSpec(memory_space=pl.ANY)],
-        out_specs=(pl.BlockSpec(memory_space=pltpu.VMEM),) * 3,
+        out_shape=(
+            shape((height, width), f32), shape((height, B), f32), shape((B, B), f32), shape((B, width), f32)
+        ),
+        in_specs=[pl.BlockSpec(memory_space=pltpu.HBM)],
+        out_specs=(pl.BlockSpec(memory_space=pltpu.VMEM),) * 4,
         scratch_shapes=[
-            pltpu.VMEM((height, width), f32),
             pltpu.VMEM((height, B), f32),
             pltpu.VMEM((B, B), f32),
             pltpu.VMEM((B, B), f32),
@@ -380,9 +381,9 @@
             dma((4, nrow)),
         ],
         compiler_params=pltpu.CompilerParams(
-            collective_id=0, has_side_effects=True, vmem_limit_bytes=60 * 2**20
+            collective_id=0, has_side_effects=True, vmem_limit_bytes=12 * 2**20
         ),
-    )(matrix)
+    )(pltpu.with_memory_space_constraint(matrix, pltpu.HBM))
     whole = pl.BlockSpec(memory_space=pltpu.VMEM)
     return pl.pallas_call(
         functools.partial(project_kernel, height * nrow),
@@ -394,8 +395,8 @@
             pltpu.VMEM((3 * B, width), jnp.bfloat16),
             dma((4,)),
         ],
-        compiler_params=pltpu.CompilerParams(vmem_limit_bytes=32 * 2**20),
-    )(matrix, basis, inverse, coeffs)
+        compiler_params=pltpu.CompilerParams(vmem_limit_bytes=12 * 2**20),
+    )(held, basis, inverse, coeffs)
 
 
 def solution(mesh):

time: 47.6 us -> 43.7 us (0.918)
  local copies, waits for them, and re-layouts: 2.83 us -> 0 us
  Pallas kernels: 43.9 us -> 43 us
    unnamed x8 -> x0, local copies, waits for them, and re-layouts: 2.83 us -> none
    pallas_call x1, Pallas kernels: 40.8 us -> 39.9 us  [on_device(): pl.pallas_call(functools.partial(kernel, nrow, ncol), out_shape=(shape((h...]
where the time goes in v1:
time: 43.7 us; the launch traced here: 43.6 us
  Pallas kernels  43 us (98%)
  between operations  0.64 us (1%)
    pallas_call x1, Pallas kernels, on_device(): pl.pallas_call(functools.partial(kernel, nrow, ncol), out_shape=(shape((h...  39.9 us
    pallas_call x1, Pallas kernels, on_device(): pl.pallas_call(functools.partial(project_kernel, height * nrow), out_shap...  3.08 us

profile of v1, /device:TPU:17, one launch (start us, length us, event | category | flops | bytes accessed | tf_op | source)
XLA Modules:
  0.0 43.6 jit_solution(3198811133154067006)
XLA Ops:
  0.6 39.9 %shard_map.30 = (f32[1024,512]{1,0:T(8,128)S(1)}, f32[1024,128]{1,0:T(8,128)S(1)}, f32[128,128]{1,0:T(8,128)S(1)}, f32[128,512]{1,0:T(8,128)S(1)}) custom-call(f32[1024,512]{1,0:T(8,128)} %m_hbm.1), custom_call_target="tpu_custom_call" | custom-call | tf_op jit(solution)/shard_map/pallas_call | solution.py:360
  40.5 3.1 %shard_map.31 = (f32[1024,512]{1,0:T(8,128)}, f32[128,512]{1,0:T(8,128)}) custom-call(f32[1024,512]{1,0:T(8,128)S(1)} %get-tuple-element.6.m_ref, f32[1024,128]{1,0:T(8,128)S(1)} %get-tuple-element.7.q_ref, f32[128,128]{1,0:T(8,128)S(1)} %get-tuple-element.8.g2_ref, f32[128,512]{1,0:T(8,128)S(1)} %get-tuple-element.9.p_ref), custom_call_target="tpu_custom_call" | custom-call | tf_op jit(solution)/shard_map/pallas_call | solution.py:388

commit v2 on v1

--- a/solution.py
+++ b/solution.py
@@ -20,23 +20,38 @@
     )
 
 
-def factor_steps(w_ref, low, high, state=None, after_step=None):
+def thirds(x):
+    high = x.astype(jnp.bfloat16).astype(jnp.float32)
+    rest = x - high
+    mid = rest.astype(jnp.bfloat16).astype(jnp.float32)
+    return high, mid, rest - mid
+
+
+def self_product(t):
+    high, mid, low = thirds(t)
+    left = jnp.concatenate([high, high, mid, mid, high, low], 0).astype(jnp.bfloat16)
+    right = jnp.concatenate([high, mid, high, mid, low, high], 0).astype(jnp.bfloat16)
+    return lax.dot_general(
+        left, right, (((0,), (0,)), ((), ())), preferred_element_type=jnp.float32
+    )
+
+
+def factor_steps(w_ref, c_ref, low, high, state=None, after_step=None):
     lane = lax.broadcasted_iota(jnp.int32, (S, B), 1)
     sub = lax.broadcasted_iota(jnp.int32, (S, B), 0)
-    wide = lax.broadcasted_iota(jnp.int32, (B - 2 * S, B), 1)
-
-    def step(k, state):
-        rows, mult, last = state
+    count = B // S
+    w = [w_ref[S * r : S * r + S] for r in range(count)] if state is None else state
+    for k in range(low, high):
+        here = (lane >= S * k) & (lane < S * k + S)
+        rows = w[k]
         d = {}
         for j in range(S):
-            column = jnp.broadcast_to(rows[:, j : j + 1], (S, B))
+            c_ref[S * j : S * j + S] = jnp.broadcast_to(
+                rows[:, S * k + j : S * k + j + 1], (S, B)
+            )
             for i in range(j, S):
-                d[i, j] = jnp.broadcast_to(column[i : i + 1], (S, B))
-        rest = w_ref[S : B - S] - mm(mult, last, ((0,), (0,)))[2 * S :]
-        rest = pltpu.roll(jnp.where(wide < S, 0.0, rest), B - S, 1)
-        w_ref[: B - 2 * S] = rest
-        w_ref[B - 2 * S : B - S] = pltpu.roll(jnp.where(lane < S, 0.0, last), B - S, 1)
-        rows = jnp.where(lane < S, jnp.where(lane == sub, 1.0, 0.0), rows)
+                d[i, j] = jnp.broadcast_to(c_ref[S * j + i : S * j + i + 1], (S, B))
+        rows = jnp.where(here, jnp.where(lane - S * k == sub, 1.0, 0.0), rows)
         p = [jnp.broadcast_to(rows[j : j + 1], (S, B)) for j in range(S)]
         t = None
         for j in range(S):
@@ -49,23 +64,22 @@
             for i in range(j + 1, S):
                 p[i] = p[i] - l[i] * tj
             t = tj if t is None else jnp.where(sub == j, tj, t)
-        mult = jnp.where((lane >= S) & (lane < B - S * k), t, 0.0)
-        last = pltpu.roll(t, B - S, 1)
-        after = rest[:S]
-        for i in range(S):
-            column = jnp.broadcast_to(mult[:, S + i : S + i + 1], (S, B))
-            drop = jnp.sum(column * last, axis=0, keepdims=True)
-            after = jnp.where(sub == i, after - drop, after)
+        w_ref[S * k : S * k + S] = jnp.where(lane < S * k + S, t, 0.0)
+        if k + 1 < count:
+            after = jnp.where(here, 0.0, w[k + 1])
+            for i in range(S):
+                at = S * (k + 1) + i
+                column = jnp.broadcast_to(t[:, at : at + 1], (S, B))
+                drop = jnp.sum(column * t, axis=0, keepdims=True)
+                after = jnp.where(sub == i, after - drop, after)
+            w[k + 1] = after
+        if k + 2 < count:
+            change = self_product(t)
+            for r in range(k + 2, count):
+                w[r] = jnp.where(here, 0.0, w[r]) - change[S * r : S * r + S]
         if after_step is not None:
             after_step(k)
-        return after, mult, last
-
-    if low == 0:
-        state = (w_ref[:S], jnp.zeros((S, B), jnp.float32), w_ref[B - S :])
-    state = lax.fori_loop(low, high, step, state)
-    if high == B // S:
-        w_ref[B - S :] = state[2]
-    return state
+    return w
 
 
 class Sum:
@@ -154,7 +168,7 @@
 
 def kernel(
     nrow, ncol, m_hbm, m_v, q_v, g2_v, p_v,
-    a_v, s1_v, s2_v, sp_v, g1_v, box1, box2, boxp,
+    a_v, s1_v, s2_v, sp_v, g1_v, c_v, box1, box2, boxp,
     in_sems, chain_sems, g_sems, sems1, sems2, semsp,
 ):
     me = lax.axis_index("row")
@@ -243,11 +257,10 @@
     first.drain()
 
     def pass_on(k):
-        @pl.when(passes_on & (k % 3 == 1) & (k < 12))
-        def _():
-            forward(4 + k // 3)
-
-    factor_steps(g1_v, 0, B // S, None, pass_on)
+        if k % 3 == 1 and k < 12:
+            pl.when(passes_on)(lambda: forward(4 + k // 3))
+
+    factor_steps(g1_v, c_v, 0, B // S, None, pass_on)
 
     big = 2 * part
 
@@ -291,10 +304,10 @@
 
     second.end()
     second.drain()
-    state = factor_steps(g2_v, 0, B // S // 2)
+    state = factor_steps(g2_v, c_v, 0, B // S // 2)
     coeffs.middle()
     coeffs.spread()
-    factor_steps(g2_v, B // S // 2, B // S, state)
+    factor_steps(g2_v, c_v, B // S // 2, B // S, state)
     coeffs.end()
     coeffs.drain()
 
@@ -370,6 +383,7 @@
             pltpu.VMEM((B, B), f32),
             pltpu.VMEM((B, width), f32),
             pltpu.VMEM((B, B), f32),
+            pltpu.VMEM((S * S, B), f32),
             pltpu.VMEM((nrow, slab, B), f32),
             pltpu.VMEM((nrow, slab, B), f32),
             pltpu.VMEM((nrow, slab, width), f32),

time: 43.7 us -> 42.5 us (0.973)
  Pallas kernels: 43 us -> 41.7 us
    pallas_call x1, Pallas kernels: 39.9 us -> 38.6 us  [on_device(): pl.pallas_call(functools.partial(kernel, nrow, ncol), out_shape=(shape((h...]
where the time goes in v2:
time: 42.5 us; the launch traced here: 42.3 us
  Pallas kernels  41.7 us (98%)
  between operations  0.64 us (2%)
    pallas_call x1, Pallas kernels, on_device(): pl.pallas_call(functools.partial(kernel, nrow, ncol), out_shape=(shape((h...  38.6 us
    pallas_call x1, Pallas kernels, on_device(): pl.pallas_call(functools.partial(project_kernel, height * nrow), out_shap...  3.08 us

profile of v2, /device:TPU:17, one launch (start us, length us, event | category | flops | bytes accessed | tf_op | source)
XLA Modules:
  0.0 42.3 jit_solution(13024958967177042885)
XLA Ops:
  0.6 38.6 %shard_map.30 = (f32[1024,512]{1,0:T(8,128)S(1)}, f32[1024,128]{1,0:T(8,128)S(1)}, f32[128,128]{1,0:T(8,128)S(1)}, f32[128,512]{1,0:T(8,128)S(1)}) custom-call(f32[1024,512]{1,0:T(8,128)} %m_hbm.1), custom_call_target="tpu_custom_call" | custom-call | tf_op jit(solution)/shard_map/pallas_call | solution.py:373
  39.3 3.1 %shard_map.31 = (f32[1024,512]{1,0:T(8,128)}, f32[128,512]{1,0:T(8,128)}) custom-call(f32[1024,512]{1,0:T(8,128)S(1)} %get-tuple-element.6.m_ref, f32[1024,128]{1,0:T(8,128)S(1)} %get-tuple-element.7.q_ref, f32[128,128]{1,0:T(8,128)S(1)} %get-tuple-element.8.g2_ref, f32[128,512]{1,0:T(8,128)S(1)} %get-tuple-element.9.p_ref), custom_call_target="tpu_custom_call" | custom-call | tf_op jit(solution)/shard_map/pallas_call | solution.py:402

commit v3 on v2

--- a/solution.py
+++ b/solution.py
@@ -11,6 +11,11 @@
 B = 128
 S = 8
 CHUNKS = 8
+EARLY = 3
+NEAR = {-1: (3, 4, 5, 6, 7)}
+LAST = 3
+COLLECT = {7: (0, 1, 2, 3)}
+FAR = {-1: (3, 4), 1: (5,), 5: (6,), 9: (7,)}
 HI = lax.Precision.HIGHEST
 
 
@@ -166,10 +171,88 @@
         self.own(self.me, sent)
 
 
+class PairSum:
+    def __init__(self, size, me, src, pair, gather, full, pair_sems, chip_sems):
+        self.chips, self.me, self.core, self.chip = size // 2, me, me % 2, me // 2
+        self.src, self.pair, self.gather, self.full = src, pair, gather, full
+        self.pair_sems, self.chip_sems = pair_sems, chip_sems
+        self.half = B // 2
+        self.parts = src.shape[1] // B
+
+    def rows(self, core):
+        return pl.ds(pl.multiple_of(core * self.half, self.half), self.half)
+
+    def swap_copy(self, c):
+        cols = pl.ds(c * B, B)
+        return pltpu.make_async_remote_copy(
+            src_ref=self.src.at[self.rows(1 - self.core), cols],
+            dst_ref=self.pair.at[:, cols],
+            send_sem=self.pair_sems.at[0, c],
+            recv_sem=self.pair_sems.at[1, c],
+            device_id={"row": self.me ^ 1},
+            device_id_type=pl.DeviceIdType.MESH,
+        )
+
+    def chip_copy(self, c, i, slot):
+        cols = pl.ds(c * B, B)
+        return pltpu.make_async_remote_copy(
+            src_ref=self.gather.at[slot, :, cols],
+            dst_ref=self.gather.at[slot, :, cols],
+            send_sem=self.chip_sems.at[0, c, i],
+            recv_sem=self.chip_sems.at[1, c, i],
+            device_id={"row": self.me ^ (2 * i)},
+            device_id_type=pl.DeviceIdType.MESH,
+        )
+
+    def back_copy(self, c, core):
+        cols = pl.ds(c * B, B)
+        return pltpu.make_async_remote_copy(
+            src_ref=self.full.at[self.rows(core), cols],
+            dst_ref=self.full.at[self.rows(core), cols],
+            send_sem=self.pair_sems.at[2, c],
+            recv_sem=self.pair_sems.at[3, c],
+            device_id={"row": self.me ^ 1},
+            device_id_type=pl.DeviceIdType.MESH,
+        )
+
+    def swap(self):
+        for c in range(self.parts):
+            self.swap_copy(c).start()
+
+    def spread(self):
+        for c in range(self.parts):
+            cols = pl.ds(c * B, B)
+            self.swap_copy(c).wait_recv()
+            self.gather[self.chip, :, cols] = self.src[self.rows(self.core), cols] + self.pair[:, cols]
+            for i in range(self.chips - 1, 0, -1):
+                self.chip_copy(c, i, self.chip).start()
+
+    def collect(self, c):
+        cols = pl.ds(c * B, B)
+        for i in range(1, self.chips):
+            self.chip_copy(c, i, self.chip ^ i).wait_recv()
+        total = self.gather[0, :, cols]
+        for i in range(1, self.chips):
+            total = total + self.gather[i, :, cols]
+        self.full[self.rows(self.core), cols] = total
+        self.back_copy(c, self.core).start()
+
+    def end(self):
+        for c in range(self.parts):
+            self.back_copy(c, 1 - self.core).wait_recv()
+
+    def drain(self):
+        for c in range(self.parts):
+            self.swap_copy(c).wait_send()
+            self.back_copy(c, self.core).wait_send()
+            for i in range(1, self.chips):
+                self.chip_copy(c, i, self.chip).wait_send()
+
+
 def kernel(
     nrow, ncol, m_hbm, m_v, q_v, g2_v, p_v,
-    a_v, s1_v, s2_v, sp_v, g1_v, c_v, box1, box2, boxp,
-    in_sems, chain_sems, g_sems, sems1, sems2, semsp,
+    a_v, s1_v, s2_v, sp_v, g1_v, c_v, box1, box2, pair_v, gather_v,
+    in_sems, chain_sems, g_sems, sems1, sems2, pair_sems, chip_sems, ready,
 ):
     me = lax.axis_index("row")
     z = lax.axis_index("col")
@@ -183,14 +266,43 @@
         pl.semaphore_signal(
             barrier, inc=1, device_id={"row": me ^ i}, device_id_type=pl.DeviceIdType.MESH
         )
-    for i in range(1, ncol):
+
+    def greet(sem, column):
         pl.semaphore_signal(
-            barrier, inc=1, device_id={"col": z ^ i}, device_id_type=pl.DeviceIdType.MESH
-        )
-
-    pl.when(z == 0)(load_a.start)
+            sem, inc=1, device_id={"col": column}, device_id_type=pl.DeviceIdType.MESH
+        )
+
+    @pl.when(z > 0)
+    def _():
+        greet(barrier, z - 1)
+
+    @pl.when(z == 0)
+    def _():
+        load_a.start()
+        for i in range(2, ncol):
+            greet(barrier, i)
+
     load_m.start()
-    pl.semaphore_wait(barrier, nrow + ncol - 2)
+
+    def enter():
+        sends_on = jnp.where(z < ncol - 1, 1, 0)
+        far = jnp.where(z > 1, 1, 0)
+        pl.semaphore_wait(barrier, nrow - 1 + sends_on + far)
+
+    first = Sum(nrow, me, s1_v, box1, g1_v, sems1)
+    second = Sum(nrow, me, s2_v, box2, g2_v, sems2)
+    coeffs = PairSum(nrow, me, sp_v, pair_v, gather_v, p_v, pair_sems, chip_sems)
+
+    @pl.when(z == 0)
+    def _():
+        load_a.wait()
+        s1_v[...] = mm(a_v[...], a_v[...], ((0,), (0,)))
+
+    enter()
+
+    @pl.when(z > 1)
+    def _():
+        greet(ready, 0)
 
     def chain(c):
         block = a_v.at[pl.ds(pl.multiple_of(c * part, part), part)]
@@ -205,13 +317,10 @@
 
     passes_on = (z > 0) & (z < ncol - 1)
 
-    def forward(c):
-        chain(c).wait_recv()
-        chain(c).start()
-
-    first = Sum(nrow, me, s1_v, box1, g1_v, sems1)
-    second = Sum(nrow, me, s2_v, box2, g2_v, sems2)
-    coeffs = Sum(nrow, me, sp_v, boxp, p_v, semsp)
+    def forward(*chunks):
+        for c in chunks:
+            chain(c).wait_recv()
+            chain(c).start()
 
     def hand(which, total, i):
         return pltpu.make_async_remote_copy(
@@ -225,41 +334,43 @@
 
     def give(which, total):
         def send():
-            for i in range(1, ncol):
+            for i in range(ncol - 1, 0, -1):
                 hand(which, total, i).start()
 
         first.own(me, send)
 
     @pl.when(z == 0)
     def _():
-        load_a.wait()
-        for c in range(3):
+        for c in range(EARLY):
             chain(c).start()
-        s1_v[...] = mm(a_v[...], a_v[...], ((0,), (0,)))
         first.start()
         first.middle()
+        if ncol > 2:
+            pl.semaphore_wait(ready, ncol - 2)
         give(0, first)
         first.spread()
-        for c in range(3, CHUNKS):
+        for c in range(EARLY, CHUNKS):
             chain(c).start()
 
     @pl.when(passes_on)
     def _():
-        for c in range(4):
-            forward(c)
+        forward(*range(EARLY))
 
     @pl.when(z > 0)
     def _():
         first.own(me, lambda: hand(0, first, 0).wait_recv())
         first.spread()
 
+    def pass_on(k):
+        near, far = NEAR.get(k, ()), FAR.get(k, ())
+        if near:
+            pl.when(passes_on & (z == 1))(lambda: forward(*near))
+        if far:
+            pl.when(passes_on & (z > 1))(lambda: forward(*far))
+
+    pass_on(-1)
     first.end()
     first.drain()
-
-    def pass_on(k):
-        if k % 3 == 1 and k < 12:
-            pl.when(passes_on)(lambda: forward(4 + k // 3))
-
     factor_steps(g1_v, c_v, 0, B // S, None, pass_on)
 
     big = 2 * part
@@ -274,18 +385,22 @@
         second.start()
         load_m.wait()
         sp_v[...] = mm(q_v[...], m_v[...], ((0,), (0,)))
+        coeffs.swap()
         second.middle()
         give(1, second)
         second.spread()
-        coeffs.start()
+        coeffs.spread()
 
     @pl.when(z > 0)
     def _():
         load_m.wait()
+        def share():
+            second.own(me, lambda: hand(1, second, 0).wait_recv())
+            second.spread()
+
         for c in range(CHUNKS // 2):
-            if c == CHUNKS // 2 - 1:
-                second.own(me, lambda: hand(1, second, 0).wait_recv())
-                second.spread()
+            if c == LAST:
+                share()
 
             @pl.when(z == ncol - 1)
             def _():
@@ -300,14 +415,20 @@
                 sp_v[...] = term
             else:
                 sp_v[...] += term
-        coeffs.start()
+        coeffs.swap()
+        coeffs.spread()
 
     second.end()
     second.drain()
-    state = factor_steps(g2_v, c_v, 0, B // S // 2)
-    coeffs.middle()
-    coeffs.spread()
-    factor_steps(g2_v, c_v, B // S // 2, B // S, state)
+
+    def collect(k):
+        for c in COLLECT.get(k, ()):
+            if c < coeffs.parts:
+                coeffs.collect(c)
+
+    factor_steps(g2_v, c_v, 0, B // S, None, collect)
+    for c in range(max(sum(COLLECT.values(), ())) + 1, coeffs.parts):
+        coeffs.collect(c)
     coeffs.end()
     coeffs.drain()
 
@@ -386,13 +507,16 @@
             pltpu.VMEM((S * S, B), f32),
             pltpu.VMEM((nrow, slab, B), f32),
             pltpu.VMEM((nrow, slab, B), f32),
-            pltpu.VMEM((nrow, slab, width), f32),
+            pltpu.VMEM((B // 2, width), f32),
+            pltpu.VMEM((nrow // 2, B // 2, width), f32),
             dma((2,)),
             dma((2, CHUNKS)),
             dma((4, ncol)),
             dma((4, nrow)),
             dma((4, nrow)),
-            dma((4, nrow)),
+            dma((4, width // B)),
+            dma((2, width // B, nrow // 2)),
+            pltpu.SemaphoreType.REGULAR,
         ],
         compiler_params=pltpu.CompilerParams(
             collective_id=0, has_side_effects=True, vmem_limit_bytes=12 * 2**20

time: 42.5 us -> 38.4 us (0.904)
  Pallas kernels: 41.7 us -> 37.4 us
    pallas_call x1, Pallas kernels: 38.6 us -> 34.4 us  [on_device(): pl.pallas_call(functools.partial(kernel, nrow, ncol), out_shape=(shape((h...]
where the time goes in v3:
time: 38.4 us; the launch traced here: 38.1 us
  Pallas kernels  37.4 us (97%)
  between operations  0.64 us (2%)
    pallas_call x1, Pallas kernels, on_device(): pl.pallas_call(functools.partial(kernel, nrow, ncol), out_shape=(shape((h...  34.4 us
    pallas_call x1, Pallas kernels, on_device(): pl.pallas_call(functools.partial(project_kernel, height * nrow), out_shap...  3.07 us

profile of v3, /device:TPU:17, one launch (start us, length us, event | category | flops | bytes accessed | tf_op | source)
XLA Modules:
  0.0 38.1 jit_solution(10215862619112335096)
XLA Ops:
  0.6 34.4 %shard_map.30 = (f32[1024,512]{1,0:T(8,128)S(1)}, f32[1024,128]{1,0:T(8,128)S(1)}, f32[128,128]{1,0:T(8,128)S(1)}, f32[128,512]{1,0:T(8,128)S(1)}) custom-call(f32[1024,512]{1,0:T(8,128)} %m_hbm.1), custom_call_target="tpu_custom_call" | custom-call | tf_op jit(solution)/shard_map/pallas_call | solution.py:494
  35.0 3.1 %shard_map.31 = (f32[1024,512]{1,0:T(8,128)}, f32[128,512]{1,0:T(8,128)}) custom-call(f32[1024,512]{1,0:T(8,128)S(1)} %get-tuple-element.6.m_ref, f32[1024,128]{1,0:T(8,128)S(1)} %get-tuple-element.7.q_ref, f32[128,128]{1,0:T(8,128)S(1)} %get-tuple-element.8.g2_ref, f32[128,512]{1,0:T(8,128)S(1)} %get-tuple-element.9.p_ref), custom_call_target="tpu_custom_call" | custom-call | tf_op jit(solution)/shard_map/pallas_call | solution.py:526

commit v4 on v3

--- a/solution.py
+++ b/solution.py
@@ -41,22 +41,28 @@
     )
 
 
-def factor_steps(w_ref, c_ref, low, high, state=None, after_step=None):
+def spread_block(c_ref, rows, k):
+    for j in range(S):
+        c_ref[S * j : S * j + S] = jnp.broadcast_to(
+            rows[:, S * k + j : S * k + j + 1], (S, B)
+        )
+    return {
+        (i, j): jnp.broadcast_to(c_ref[S * j + i : S * j + i + 1], (S, B))
+        for j in range(S)
+        for i in range(j, S)
+    }
+
+
+def factor_steps(w_ref, c_ref, after_step):
     lane = lax.broadcasted_iota(jnp.int32, (S, B), 1)
     sub = lax.broadcasted_iota(jnp.int32, (S, B), 0)
     count = B // S
-    w = [w_ref[S * r : S * r + S] for r in range(count)] if state is None else state
-    for k in range(low, high):
+    w = [w_ref[S * r : S * r + S] for r in range(count)]
+    d = spread_block(c_ref, w[0], 0)
+    for k in range(count):
         here = (lane >= S * k) & (lane < S * k + S)
-        rows = w[k]
-        d = {}
-        for j in range(S):
-            c_ref[S * j : S * j + S] = jnp.broadcast_to(
-                rows[:, S * k + j : S * k + j + 1], (S, B)
-            )
-            for i in range(j, S):
-                d[i, j] = jnp.broadcast_to(c_ref[S * j + i : S * j + i + 1], (S, B))
-        rows = jnp.where(here, jnp.where(lane - S * k == sub, 1.0, 0.0), rows)
+        following = spread_block(c_ref, w[k + 1], k + 1) if k + 1 < count else None
+        rows = jnp.where(here, jnp.where(lane - S * k == sub, 1.0, 0.0), w[k])
         p = [jnp.broadcast_to(rows[j : j + 1], (S, B)) for j in range(S)]
         t = None
         for j in range(S):
@@ -71,20 +77,25 @@
             t = tj if t is None else jnp.where(sub == j, tj, t)
         w_ref[S * k : S * k + S] = jnp.where(lane < S * k + S, t, 0.0)
         if k + 1 < count:
+            at = S * (k + 1)
+            columns = [jnp.broadcast_to(t[:, at + i : at + i + 1], (S, B)) for i in range(S)]
+
+            def drop(i, what):
+                return jnp.sum(columns[i] * what, axis=0, keepdims=True)
+
+            d = {
+                (i, j): following[i, j] - jnp.broadcast_to(drop(i, columns[j]), (S, B))
+                for (i, j) in following
+            }
             after = jnp.where(here, 0.0, w[k + 1])
             for i in range(S):
-                at = S * (k + 1) + i
-                column = jnp.broadcast_to(t[:, at : at + 1], (S, B))
-                drop = jnp.sum(column * t, axis=0, keepdims=True)
-                after = jnp.where(sub == i, after - drop, after)
+                after = jnp.where(sub == i, after - drop(i, t), after)
             w[k + 1] = after
         if k + 2 < count:
             change = self_product(t)
             for r in range(k + 2, count):
                 w[r] = jnp.where(here, 0.0, w[r]) - change[S * r : S * r + S]
-        if after_step is not None:
-            after_step(k)
-    return w
+        after_step(k)
 
 
 class Sum:
@@ -371,7 +382,7 @@
     pass_on(-1)
     first.end()
     first.drain()
-    factor_steps(g1_v, c_v, 0, B // S, None, pass_on)
+    factor_steps(g1_v, c_v, pass_on)
 
     big = 2 * part
 
@@ -426,7 +437,7 @@
             if c < coeffs.parts:
                 coeffs.collect(c)
 
-    factor_steps(g2_v, c_v, 0, B // S, None, collect)
+    factor_steps(g2_v, c_v, collect)
     for c in range(max(sum(COLLECT.values(), ())) + 1, coeffs.parts):
         coeffs.collect(c)
     coeffs.end()
@@ -452,14 +463,13 @@
     return high, (x - high.astype(jnp.float32)).astype(jnp.bfloat16)
 
 
-def project_kernel(rows, m_ref, q_ref, g2_ref, p_ref, out_hbm, top_ref, out_v, back_v, sems):
+def project_kernel(rows, m_ref, q_ref, g2_ref, p_ref, out_hbm, top_hbm, out_v, top_v, back_v, sems):
     height, width = m_ref.shape
     part = height // 4
     scale = math.sqrt(rows)
     on_panel = lax.axis_index("col") == 0
     g2 = g2_ref[...]
     c = mm(g2, p_ref[...], ((1,), (0,)))
-    top_ref[...] = c / scale
     back = mm(g2, c, ((0,), (0,)))
     leading = jnp.where(on_panel, -scale * g2.T, back[:, :B])
     high, low = halves(jnp.concatenate([leading, back[:, B:]], 1))
@@ -467,6 +477,10 @@
     back_v[B : 2 * B] = high
     back_v[2 * B :] = low
 
+    top_v[...] = c / scale
+    top_store = pltpu.make_async_copy(top_v, top_hbm, sems.at[4])
+    top_store.start()
+
     def store(i):
         block = pl.ds(i * part, part)
         return pltpu.make_async_copy(out_v.at[block], out_hbm.at[block], sems.at[i])
@@ -481,6 +495,7 @@
         out_v[block, :B] = jnp.where(on_panel, 0.0, base[:, :B]) - change[:, :B]
         out_v[block, B:] = base[:, B:] - change[:, B:]
         store(i).start()
+    top_store.wait()
     for i in range(4):
         store(i).wait()
 
@@ -527,11 +542,12 @@
         functools.partial(project_kernel, height * nrow),
         out_shape=(shape((height, width), f32), shape((B, width), f32)),
         in_specs=[whole] * 4,
-        out_specs=(pl.BlockSpec(memory_space=pl.ANY), whole),
+        out_specs=(pl.BlockSpec(memory_space=pl.ANY),) * 2,
         scratch_shapes=[
             pltpu.VMEM((height, width), f32),
+            pltpu.VMEM((B, width), f32),
             pltpu.VMEM((3 * B, width), jnp.bfloat16),
-            dma((4,)),
+            dma((5,)),
         ],
         compiler_params=pltpu.CompilerParams(vmem_limit_bytes=12 * 2**20),
     )(held, basis, inverse, coeffs)

time: 38.4 us -> 37.3 us (0.971)
  Pallas kernels: 37.4 us -> 36 us
    pallas_call x1, Pallas kernels: 34.4 us -> 33.6 us  [on_device(): pl.pallas_call(functools.partial(kernel, nrow, ncol), out_shape=(shape((h...]
    pallas_call x1, Pallas kernels: 3.07 us -> 2.38 us  [on_device(): pl.pallas_call(functools.partial(project_kernel, height * nrow), out_shap...]
where the time goes in v4:
time: 37.3 us; the launch traced here: 36.6 us
  Pallas kernels  36 us (97%)
  between operations  0.64 us (2%)
    pallas_call x1, Pallas kernels, on_device(): pl.pallas_call(functools.partial(kernel, nrow, ncol), out_shape=(shape((h...  33.6 us
    pallas_call x1, Pallas kernels, on_device(): pl.pallas_call(functools.partial(project_kernel, height * nrow), out_shap...  2.38 us

profile of v4, /device:TPU:17, one launch (start us, length us, event | category | flops | bytes accessed | tf_op | source)
XLA Modules:
  0.0 36.6 jit_solution(13822591847583981062)
XLA Ops:
  0.6 33.6 %shard_map.30 = (f32[1024,512]{1,0:T(8,128)S(1)}, f32[1024,128]{1,0:T(8,128)S(1)}, f32[128,128]{1,0:T(8,128)S(1)}, f32[128,512]{1,0:T(8,128)S(1)}) custom-call(f32[1024,512]{1,0:T(8,128)} %m_hbm.1), custom_call_target="tpu_custom_call" | custom-call | tf_op jit(solution)/shard_map/pallas_call | solution.py:509
  34.3 2.4 %shard_map.31 = (f32[1024,512]{1,0:T(8,128)}, f32[128,512]{1,0:T(8,128)}) custom-call(f32[1024,512]{1,0:T(8,128)S(1)} %get-tuple-element.6.m_ref, f32[1024,128]{1,0:T(8,128)S(1)} %get-tuple-element.7.q_ref, f32[128,128]{1,0:T(8,128)S(1)} %get-tuple-element.8.g2_ref, f32[128,512]{1,0:T(8,128)S(1)} %get-tuple-element.9.p_ref), custom_call_target="tpu_custom_call" | custom-call | tf_op jit(solution)/shard_map/pallas_call | solution.py:541

commit v5 on v4

--- a/solution.py
+++ b/solution.py
@@ -10,12 +10,16 @@
 
 B = 128
 S = 8
-CHUNKS = 8
+CUTS = (0, 2, 4, 6, 8, 10, 12, 13, 14, 15, 16)
+CHUNKS = len(CUTS) - 1
 EARLY = 3
-NEAR = {-1: (3, 4, 5, 6, 7)}
-LAST = 3
-COLLECT = {7: (0, 1, 2, 3)}
-FAR = {-1: (3, 4), 1: (5,), 5: (6,), 9: (7,)}
+NEAR = {-1: (3, 4), 0: (5,), 4: (6, 7), 9: (8, 9)}
+LAST = 2
+COLLECT_REST = {7: (0,), 11: (1,), 15: (2, 3)}
+COLLECT_LAST = {7: (0,), 11: (1,), 15: (2, 3)}
+NEXT = 5
+START = {0: (5, 6, 7), 5: (8, 9)}
+FAR = {-1: (3, 4), 1: (5,), 4: (6,), 6: (7,), 8: (8,), 10: (9,)}
 HI = lax.Precision.HIGHEST
 
 
@@ -238,15 +242,16 @@
             for i in range(self.chips - 1, 0, -1):
                 self.chip_copy(c, i, self.chip).start()
 
-    def collect(self, c):
-        cols = pl.ds(c * B, B)
-        for i in range(1, self.chips):
-            self.chip_copy(c, i, self.chip ^ i).wait_recv()
-        total = self.gather[0, :, cols]
-        for i in range(1, self.chips):
-            total = total + self.gather[i, :, cols]
-        self.full[self.rows(self.core), cols] = total
-        self.back_copy(c, self.core).start()
+    def collect(self, *parts):
+        for c in parts:
+            cols = pl.ds(c * B, B)
+            for i in range(1, self.chips):
+                self.chip_copy(c, i, self.chip ^ i).wait_recv()
+            total = self.gather[0, :, cols]
+            for i in range(1, self.chips):
+                total = total + self.gather[i, :, cols]
+            self.full[self.rows(self.core), cols] = total
+            self.back_copy(c, self.core).start()
 
     def end(self):
         for c in range(self.parts):
@@ -268,7 +273,7 @@
     me = lax.axis_index("row")
     z = lax.axis_index("col")
     height = m_v.shape[0]
-    part = height // CHUNKS
+    unit = height // CUTS[-1]
     load_m = pltpu.make_async_copy(m_hbm, m_v, in_sems.at[0])
     load_a = pltpu.make_async_copy(m_hbm.at[:, pl.ds(0, B)], a_v, in_sems.at[1])
 
@@ -316,7 +321,7 @@
         greet(ready, 0)
 
     def chain(c):
-        block = a_v.at[pl.ds(pl.multiple_of(c * part, part), part)]
+        block = a_v.at[pl.ds(CUTS[c] * unit, (CUTS[c + 1] - CUTS[c]) * unit)]
         return pltpu.make_async_remote_copy(
             src_ref=block,
             dst_ref=block,
@@ -360,7 +365,7 @@
             pl.semaphore_wait(ready, ncol - 2)
         give(0, first)
         first.spread()
-        for c in range(EARLY, CHUNKS):
+        for c in range(EARLY, NEXT):
             chain(c).start()
 
     @pl.when(passes_on)
@@ -372,8 +377,15 @@
         first.own(me, lambda: hand(0, first, 0).wait_recv())
         first.spread()
 
+    def send(*chunks):
+        for c in chunks:
+            chain(c).start()
+
     def pass_on(k):
         near, far = NEAR.get(k, ()), FAR.get(k, ())
+        starts = START.get(k, ())
+        if starts:
+            pl.when(z == 0)(lambda: send(*starts))
         if near:
             pl.when(passes_on & (z == 1))(lambda: forward(*near))
         if far:
@@ -384,11 +396,11 @@
     first.drain()
     factor_steps(g1_v, c_v, pass_on)
 
-    big = 2 * part
+    big = 4 * unit
 
     @pl.when(z == 0)
     def _():
-        for c in range(CHUNKS // 2):
+        for c in range(CUTS[-1] // 4):
             rows = pl.ds(c * big, big)
             q_v[rows] = mm(a_v[rows], g1_v[...], ((1,), (1,)))
         q = q_v[...]
@@ -409,14 +421,15 @@
             second.own(me, lambda: hand(1, second, 0).wait_recv())
             second.spread()
 
-        for c in range(CHUNKS // 2):
+        for c in range(CUTS[-1] // 4):
             if c == LAST:
                 share()
 
             @pl.when(z == ncol - 1)
             def _():
-                chain(2 * c).wait_recv()
-                chain(2 * c + 1).wait_recv()
+                for i in range(CHUNKS):
+                    if 4 * c <= CUTS[i] < 4 * c + 4:
+                        chain(i).wait_recv()
 
             rows = pl.ds(c * big, big)
             q = mm(a_v[rows], g1_v[...], ((1,), (1,)))
@@ -433,13 +446,13 @@
     second.drain()
 
     def collect(k):
-        for c in COLLECT.get(k, ()):
-            if c < coeffs.parts:
-                coeffs.collect(c)
+        rest, last = COLLECT_REST.get(k, ()), COLLECT_LAST.get(k, ())
+        if rest:
+            pl.when(z < ncol - 1)(lambda: coeffs.collect(*rest))
+        if last:
+            pl.when(z == ncol - 1)(lambda: coeffs.collect(*last))
 
     factor_steps(g2_v, c_v, collect)
-    for c in range(max(sum(COLLECT.values(), ())) + 1, coeffs.parts):
-        coeffs.collect(c)
     coeffs.end()
     coeffs.drain()
 

time: 37.3 us -> 36.3 us (0.973); the launches traced: 36.6 us -> 36.1 us
  Pallas kernels: 36 us -> 35.5 us
    pallas_call x1, Pallas kernels: 33.6 us -> 33.1 us  [on_device(): pl.pallas_call(functools.partial(kernel, nrow, ncol), out_shape=(shape((h...]
where the time goes in v5:
time: 36.3 us; the launch traced here: 36.1 us
  Pallas kernels  35.5 us (98%)
  between operations  0.64 us (2%)
    pallas_call x1, Pallas kernels, on_device(): pl.pallas_call(functools.partial(kernel, nrow, ncol), out_shape=(shape((h...  33.1 us
    pallas_call x1, Pallas kernels, on_device(): pl.pallas_call(functools.partial(project_kernel, height * nrow), out_shap...  2.37 us

profile of v5, /device:TPU:17, one launch (start us, length us, event | category | flops | bytes accessed | tf_op | source)
XLA Modules:
  0.0 36.1 jit_solution(12316336127265686688)
XLA Ops:
  0.6 33.1 %shard_map.30 = (f32[1024,512]{1,0:T(8,128)S(1)}, f32[1024,128]{1,0:T(8,128)S(1)}, f32[128,128]{1,0:T(8,128)S(1)}, f32[128,512]{1,0:T(8,128)S(1)}) custom-call(f32[1024,512]{1,0:T(8,128)} %m_hbm.1), custom_call_target="tpu_custom_call" | custom-call | tf_op jit(solution)/shard_map/pallas_call | solution.py:522
  33.8 2.4 %shard_map.31 = (f32[1024,512]{1,0:T(8,128)}, f32[128,512]{1,0:T(8,128)}) custom-call(f32[1024,512]{1,0:T(8,128)S(1)} %get-tuple-element.6.m_ref, f32[1024,128]{1,0:T(8,128)S(1)} %get-tuple-element.7.q_ref, f32[128,128]{1,0:T(8,128)S(1)} %get-tuple-element.8.g2_ref, f32[128,512]{1,0:T(8,128)S(1)} %get-tuple-element.9.p_ref), custom_call_target="tpu_custom_call" | custom-call | tf_op jit(solution)/shard_map/pallas_call | solution.py:554

commit v6 on v5

--- a/solution.py
+++ b/solution.py
@@ -15,8 +15,6 @@
 EARLY = 3
 NEAR = {-1: (3, 4), 0: (5,), 4: (6, 7), 9: (8, 9)}
 LAST = 2
-COLLECT_REST = {7: (0,), 11: (1,), 15: (2, 3)}
-COLLECT_LAST = {7: (0,), 11: (1,), 15: (2, 3)}
 NEXT = 5
 START = {0: (5, 6, 7), 5: (8, 9)}
 FAR = {-1: (3, 4), 1: (5,), 4: (6,), 6: (7,), 8: (8,), 10: (9,)}
@@ -187,12 +185,13 @@
 
 
 class PairSum:
-    def __init__(self, size, me, src, pair, gather, full, pair_sems, chip_sems):
-        self.chips, self.me, self.core, self.chip = size // 2, me, me % 2, me // 2
-        self.src, self.pair, self.gather, self.full = src, pair, gather, full
+    def __init__(self, steps, me, src, pair, gather, inbox, full, pair_sems, chip_sems):
+        self.steps, self.me, self.core = steps, me, me % 2
+        self.src, self.pair, self.gather, self.inbox, self.full = src, pair, gather, inbox, full
         self.pair_sems, self.chip_sems = pair_sems, chip_sems
         self.half = B // 2
         self.parts = src.shape[1] // B
+        self.order = sorted(range(self.parts), key=lambda c: c % (self.parts // self.steps))
 
     def rows(self, core):
         return pl.ds(pl.multiple_of(core * self.half, self.half), self.half)
@@ -208,14 +207,15 @@
             device_id_type=pl.DeviceIdType.MESH,
         )
 
-    def chip_copy(self, c, i, slot):
+    def chip_copy(self, c, step):
         cols = pl.ds(c * B, B)
-        return pltpu.make_async_remote_copy(
-            src_ref=self.gather.at[slot, :, cols],
-            dst_ref=self.gather.at[slot, :, cols],
-            send_sem=self.chip_sems.at[0, c, i],
-            recv_sem=self.chip_sems.at[1, c, i],
-            device_id={"row": self.me ^ (2 * i)},
+        turn = (step + c * self.steps // self.parts) % self.steps
+        return pltpu.make_async_remote_copy(
+            src_ref=self.gather.at[step, :, cols],
+            dst_ref=self.inbox.at[step, :, cols],
+            send_sem=self.chip_sems.at[0, c, step],
+            recv_sem=self.chip_sems.at[1, c, step],
+            device_id={"row": self.me ^ (2 << turn)},
             device_id_type=pl.DeviceIdType.MESH,
         )
 
@@ -235,22 +235,30 @@
             self.swap_copy(c).start()
 
     def spread(self):
-        for c in range(self.parts):
+        for c in self.order:
             cols = pl.ds(c * B, B)
             self.swap_copy(c).wait_recv()
-            self.gather[self.chip, :, cols] = self.src[self.rows(self.core), cols] + self.pair[:, cols]
-            for i in range(self.chips - 1, 0, -1):
-                self.chip_copy(c, i, self.chip).start()
-
-    def collect(self, *parts):
-        for c in parts:
+            self.gather[0, :, cols] = self.src[self.rows(self.core), cols] + self.pair[:, cols]
+            self.chip_copy(c, 0).start()
+
+    def relay(self):
+        for step in range(1, self.steps):
+            for c in self.order:
+                cols = pl.ds(c * B, B)
+                self.chip_copy(c, step - 1).wait_recv()
+                self.gather[step, :, cols] = (
+                    self.gather[step - 1, :, cols] + self.inbox[step - 1, :, cols]
+                )
+                self.chip_copy(c, step).start()
+
+    def collect(self):
+        last = self.steps - 1
+        for c in self.order:
             cols = pl.ds(c * B, B)
-            for i in range(1, self.chips):
-                self.chip_copy(c, i, self.chip ^ i).wait_recv()
-            total = self.gather[0, :, cols]
-            for i in range(1, self.chips):
-                total = total + self.gather[i, :, cols]
-            self.full[self.rows(self.core), cols] = total
+            self.chip_copy(c, last).wait_recv()
+            self.full[self.rows(self.core), cols] = (
+                self.gather[last, :, cols] + self.inbox[last, :, cols]
+            )
             self.back_copy(c, self.core).start()
 
     def end(self):
@@ -261,13 +269,13 @@
         for c in range(self.parts):
             self.swap_copy(c).wait_send()
             self.back_copy(c, self.core).wait_send()
-            for i in range(1, self.chips):
-                self.chip_copy(c, i, self.chip).wait_send()
+            for step in range(self.steps):
+                self.chip_copy(c, step).wait_send()
 
 
 def kernel(
     nrow, ncol, m_hbm, m_v, q_v, g2_v, p_v,
-    a_v, s1_v, s2_v, sp_v, g1_v, c_v, box1, box2, pair_v, gather_v,
+    a_v, s1_v, s2_v, sp_v, g1_v, c_v, box1, box2, pair_v, gather_v, inbox_v,
     in_sems, chain_sems, g_sems, sems1, sems2, pair_sems, chip_sems, ready,
 ):
     me = lax.axis_index("row")
@@ -307,7 +315,8 @@
 
     first = Sum(nrow, me, s1_v, box1, g1_v, sems1)
     second = Sum(nrow, me, s2_v, box2, g2_v, sems2)
-    coeffs = PairSum(nrow, me, sp_v, pair_v, gather_v, p_v, pair_sems, chip_sems)
+    steps = gather_v.shape[0]
+    coeffs = PairSum(steps, me, sp_v, pair_v, gather_v, inbox_v, p_v, pair_sems, chip_sems)
 
     @pl.when(z == 0)
     def _():
@@ -442,17 +451,12 @@
         coeffs.swap()
         coeffs.spread()
 
+    coeffs.relay()
     second.end()
     second.drain()
 
-    def collect(k):
-        rest, last = COLLECT_REST.get(k, ()), COLLECT_LAST.get(k, ())
-        if rest:
-            pl.when(z < ncol - 1)(lambda: coeffs.collect(*rest))
-        if last:
-            pl.when(z == ncol - 1)(lambda: coeffs.collect(*last))
-
-    factor_steps(g2_v, c_v, collect)
+    factor_steps(g2_v, c_v, lambda k: None)
+    coeffs.collect()
     coeffs.end()
     coeffs.drain()
 
@@ -516,6 +520,7 @@
 def on_device(nrow, ncol, matrix):
     height, width = matrix.shape
     slab = max(8, B // nrow)
+    steps = (nrow // 2).bit_length() - 1
     f32 = jnp.float32
     dma = pltpu.SemaphoreType.DMA
     shape = jax.ShapeDtypeStruct
@@ -536,14 +541,15 @@
             pltpu.VMEM((nrow, slab, B), f32),
             pltpu.VMEM((nrow, slab, B), f32),
             pltpu.VMEM((B // 2, width), f32),
-            pltpu.VMEM((nrow // 2, B // 2, width), f32),
+            pltpu.VMEM((steps, B // 2, width), f32),
+            pltpu.VMEM((steps, B // 2, width), f32),
             dma((2,)),
             dma((2, CHUNKS)),
             dma((4, ncol)),
             dma((4, nrow)),
             dma((4, nrow)),
             dma((4, width // B)),
-            dma((2, width // B, nrow // 2)),
+            dma((2, width // B, steps)),
             pltpu.SemaphoreType.REGULAR,
         ],
         compiler_params=pltpu.CompilerParams(

time: 36.3 us -> 35.5 us (0.978)
  Pallas kernels: 35.5 us -> 34.7 us
    pallas_call x1, Pallas kernels: 33.1 us -> 32.3 us  [on_device(): pl.pallas_call(functools.partial(kernel, nrow, ncol), out_shape=(shape((h...]
where the time goes in v6:
time: 35.5 us; the launch traced here: 35.3 us
  Pallas kernels  34.7 us (98%)
  between operations  0.64 us (2%)
    pallas_call x1, Pallas kernels, on_device(): pl.pallas_call(functools.partial(kernel, nrow, ncol), out_shape=(shape((h...  32.3 us
    pallas_call x1, Pallas kernels, on_device(): pl.pallas_call(functools.partial(project_kernel, height * nrow), out_shap...  2.37 us

profile of v6, /device:TPU:17, one launch (start us, length us, event | category | flops | bytes accessed | tf_op | source)
XLA Modules:
  0.0 35.3 jit_solution(5951849889756955556)
XLA Ops:
  0.6 32.3 %shard_map.30 = (f32[1024,512]{1,0:T(8,128)S(1)}, f32[1024,128]{1,0:T(8,128)S(1)}, f32[128,128]{1,0:T(8,128)S(1)}, f32[128,512]{1,0:T(8,128)S(1)}) custom-call(f32[1024,512]{1,0:T(8,128)} %m_hbm.1), custom_call_target="tpu_custom_call" | custom-call | tf_op jit(solution)/shard_map/pallas_call | solution.py:527
  32.9 2.4 %shard_map.31 = (f32[1024,512]{1,0:T(8,128)}, f32[128,512]{1,0:T(8,128)}) custom-call(f32[1024,512]{1,0:T(8,128)S(1)} %get-tuple-element.6.m_ref, f32[1024,128]{1,0:T(8,128)S(1)} %get-tuple-element.7.q_ref, f32[128,128]{1,0:T(8,128)S(1)} %get-tuple-element.8.g2_ref, f32[128,512]{1,0:T(8,128)S(1)} %get-tuple-element.9.p_ref), custom_call_target="tpu_custom_call" | custom-call | tf_op jit(solution)/shard_map/pallas_call | solution.py:560

commit v7 on v6

--- a/solution.py
+++ b/solution.py
@@ -231,7 +231,7 @@
         )
 
     def swap(self):
-        for c in range(self.parts):
+        for c in self.order:
             self.swap_copy(c).start()
 
     def spread(self):
@@ -274,8 +274,8 @@
 
 
 def kernel(
-    nrow, ncol, m_hbm, m_v, q_v, g2_v, p_v,
-    a_v, s1_v, s2_v, sp_v, g1_v, c_v, box1, box2, pair_v, gather_v, inbox_v,
+    nrow, ncol, m_hbm, m_v, split_v, g2_v, both_v, p_v,
+    q_v, a_v, s1_v, s2_v, sp_v, g1_v, c_v, box1, box2, pair_v, gather_v, inbox_v,
     in_sems, chain_sems, g_sems, sems1, sems2, pair_sems, chip_sems, ready,
 ):
     me = lax.axis_index("row")
@@ -451,11 +451,16 @@
         coeffs.swap()
         coeffs.spread()
 
+    for c in range(CUTS[-1] // 4):
+        rows = pl.ds(c * big, big)
+        high, low = halves(q_v[rows])
+        split_v[rows] = jnp.concatenate([high, low, high], 1)
     coeffs.relay()
     second.end()
     second.drain()
 
     factor_steps(g2_v, c_v, lambda k: None)
+    both_v[...] = mm(g2_v[...], g2_v[...], ((0,), (0,)))
     coeffs.collect()
     coeffs.end()
     coeffs.drain()
@@ -480,21 +485,20 @@
     return high, (x - high.astype(jnp.float32)).astype(jnp.bfloat16)
 
 
-def project_kernel(rows, m_ref, q_ref, g2_ref, p_ref, out_hbm, top_hbm, out_v, top_v, back_v, sems):
+def project_kernel(rows, m_ref, split_ref, g2_ref, both_ref, p_ref, out_hbm, top_hbm, out_v, top_v, back_v, sems):
     height, width = m_ref.shape
     part = height // 4
     scale = math.sqrt(rows)
     on_panel = lax.axis_index("col") == 0
     g2 = g2_ref[...]
-    c = mm(g2, p_ref[...], ((1,), (0,)))
-    back = mm(g2, c, ((0,), (0,)))
+    back = mm(both_ref[...], p_ref[...], ((1,), (0,)))
     leading = jnp.where(on_panel, -scale * g2.T, back[:, :B])
     high, low = halves(jnp.concatenate([leading, back[:, B:]], 1))
     back_v[:B] = high
     back_v[B : 2 * B] = high
     back_v[2 * B :] = low
 
-    top_v[...] = c / scale
+    top_v[...] = mm(g2, p_ref[...], ((1,), (0,))) / scale
     top_store = pltpu.make_async_copy(top_v, top_hbm, sems.at[4])
     top_store.start()
 
@@ -504,9 +508,8 @@
 
     for i in range(4):
         block = pl.ds(i * part, part)
-        high, low = halves(q_ref[block])
         change = jnp.dot(
-            jnp.concatenate([high, low, high], 1), back_v[...], preferred_element_type=jnp.float32
+            split_ref[block], back_v[...], preferred_element_type=jnp.float32
         )
         base = m_ref[block]
         out_v[block, :B] = jnp.where(on_panel, 0.0, base[:, :B]) - change[:, :B]
@@ -524,14 +527,16 @@
     f32 = jnp.float32
     dma = pltpu.SemaphoreType.DMA
     shape = jax.ShapeDtypeStruct
-    held, basis, inverse, coeffs = pl.pallas_call(
+    held, basis, inverse, both, coeffs = pl.pallas_call(
         functools.partial(kernel, nrow, ncol),
         out_shape=(
-            shape((height, width), f32), shape((height, B), f32), shape((B, B), f32), shape((B, width), f32)
+            shape((height, width), f32), shape((height, 3 * B), jnp.bfloat16),
+            shape((B, B), f32), shape((B, B), f32), shape((B, width), f32)
         ),
         in_specs=[pl.BlockSpec(memory_space=pltpu.HBM)],
-        out_specs=(pl.BlockSpec(memory_space=pltpu.VMEM),) * 4,
+        out_specs=(pl.BlockSpec(memory_space=pltpu.VMEM),) * 5,
         scratch_shapes=[
+            pltpu.VMEM((height, B), f32),
             pltpu.VMEM((height, B), f32),
             pltpu.VMEM((B, B), f32),
             pltpu.VMEM((B, B), f32),
@@ -560,7 +565,7 @@
     return pl.pallas_call(
         functools.partial(project_kernel, height * nrow),
         out_shape=(shape((height, width), f32), shape((B, width), f32)),
-        in_specs=[whole] * 4,
+        in_specs=[whole] * 5,
         out_specs=(pl.BlockSpec(memory_space=pl.ANY),) * 2,
         scratch_shapes=[
             pltpu.VMEM((height, width), f32),
@@ -569,7 +574,7 @@
             dma((5,)),
         ],
         compiler_params=pltpu.CompilerParams(vmem_limit_bytes=12 * 2**20),
-    )(held, basis, inverse, coeffs)
+    )(held, basis, inverse, both, coeffs)
 
 
 def solution(mesh):

time: 35.5 us -> 35.2 us (level)
  no operation moved by 1% of the time
where the time goes in v7:
time: 35.2 us; the launch traced here: 35 us
  Pallas kernels  34.4 us (98%)
  between operations  0.64 us (2%)
    pallas_call x1, Pallas kernels, on_device(): pl.pallas_call(functools.partial(kernel, nrow, ncol), out_shape=(shape((h...  32.3 us
    pallas_call x1, Pallas kernels, on_device(): pl.pallas_call(functools.partial(project_kernel, height * nrow), out_shap...  2.07 us

profile of v7, /device:TPU:17, one launch (start us, length us, event | category | flops | bytes accessed | tf_op | source)
XLA Modules:
  0.0 35.0 jit_solution(12733720615465752939)
XLA Ops:
  0.6 32.3 %shard_map.30 = (f32[1024,512]{1,0:T(8,128)S(1)}, bf16[1024,384]{1,0:T(8,128)(2,1)S(1)}, f32[128,128]{1,0:T(8,128)S(1)}, f32[128,128]{1,0:T(8,128)S(1)}, f32[128,512]{1,0:T(8,128)S(1)}) custom-call(f32[1024,512]{1,0:T(8,128)} %m_hbm.1), custom_call_target="tpu_custom_call" | custom-call | tf_op jit(solution)/shard_map/pallas_call | solution.py:530
  32.9 2.1 %shard_map.31 = (f32[1024,512]{1,0:T(8,128)}, f32[128,512]{1,0:T(8,128)}) custom-call(f32[1024,512]{1,0:T(8,128)S(1)} %get-tuple-element.7.m_ref, bf16[1024,384]{1,0:T(8,128)(2,1)S(1)} %get-tuple-element.8.split_ref, f32[128,128]{1,0:T(8,128)S(1)} %get-tuple-element.9.g2_ref, f32[128,128]{1,0:T(8,128)S(1)} %get-tuple-element.10.both_ref, ...), custom_call_target="tpu_custom_call" | custom-call | tf_op jit(solution)/shard_map/pallas_call | solution.py:565

commit v8 on v7

--- a/solution.py
+++ b/solution.py
@@ -487,7 +487,7 @@
 
 def project_kernel(rows, m_ref, split_ref, g2_ref, both_ref, p_ref, out_hbm, top_hbm, out_v, top_v, back_v, sems):
     height, width = m_ref.shape
-    part = height // 4
+    part = height // 8
     scale = math.sqrt(rows)
     on_panel = lax.axis_index("col") == 0
     g2 = g2_ref[...]
@@ -499,14 +499,14 @@
     back_v[2 * B :] = low
 
     top_v[...] = mm(g2, p_ref[...], ((1,), (0,))) / scale
-    top_store = pltpu.make_async_copy(top_v, top_hbm, sems.at[4])
+    top_store = pltpu.make_async_copy(top_v, top_hbm, sems.at[8])
     top_store.start()
 
     def store(i):
         block = pl.ds(i * part, part)
         return pltpu.make_async_copy(out_v.at[block], out_hbm.at[block], sems.at[i])
 
-    for i in range(4):
+    for i in range(8):
         block = pl.ds(i * part, part)
         change = jnp.dot(
             split_ref[block], back_v[...], preferred_element_type=jnp.float32
@@ -516,7 +516,7 @@
         out_v[block, B:] = base[:, B:] - change[:, B:]
         store(i).start()
     top_store.wait()
-    for i in range(4):
+    for i in range(8):
         store(i).wait()
 
 
@@ -571,7 +571,7 @@
             pltpu.VMEM((height, width), f32),
             pltpu.VMEM((B, width), f32),
             pltpu.VMEM((3 * B, width), jnp.bfloat16),
-            dma((5,)),
+            dma((9,)),
         ],
         compiler_params=pltpu.CompilerParams(vmem_limit_bytes=12 * 2**20),
     )(held, basis, inverse, both, coeffs)

time: 35.2 us -> 35.1 us (level)
  no operation moved by 1% of the time
where the time goes in v8:
time: 35.1 us; the launch traced here: 35 us
  Pallas kernels  34.4 us (98%)
  between operations  0.64 us (2%)
    pallas_call x1, Pallas kernels, on_device(): pl.pallas_call(functools.partial(kernel, nrow, ncol), out_shape=(shape((h...  32.3 us
    pallas_call x1, Pallas kernels, on_device(): pl.pallas_call(functools.partial(project_kernel, height * nrow), out_shap...  2.05 us

profile of v8, /device:TPU:17, one launch (start us, length us, event | category | flops | bytes accessed | tf_op | source)
XLA Modules:
  0.0 35.0 jit_solution(11555440620665782574)
XLA Ops:
  0.6 32.3 %shard_map.30 = (f32[1024,512]{1,0:T(8,128)S(1)}, bf16[1024,384]{1,0:T(8,128)(2,1)S(1)}, f32[128,128]{1,0:T(8,128)S(1)}, f32[128,128]{1,0:T(8,128)S(1)}, f32[128,512]{1,0:T(8,128)S(1)}) custom-call(f32[1024,512]{1,0:T(8,128)} %m_hbm.1), custom_call_target="tpu_custom_call" | custom-call | tf_op jit(solution)/shard_map/pallas_call | solution.py:530
  32.9 2.0 %shard_map.31 = (f32[1024,512]{1,0:T(8,128)}, f32[128,512]{1,0:T(8,128)}) custom-call(f32[1024,512]{1,0:T(8,128)S(1)} %get-tuple-element.7.m_ref, bf16[1024,384]{1,0:T(8,128)(2,1)S(1)} %get-tuple-element.8.split_ref, f32[128,128]{1,0:T(8,128)S(1)} %get-tuple-element.9.g2_ref, f32[128,128]{1,0:T(8,128)S(1)} %get-tuple-element.10.both_ref, ...), custom_call_target="tpu_custom_call" | custom-call | tf_op jit(solution)/shard_map/pallas_call | solution.py:565
